TPU v7x, 256 devices: a whole 4x4x8 slice. The times are simulated.
256 devices in a mesh: replica: 64 (over z, y, x_lo), fsdp: 4 (over x_hi, core).
Axes of the slice: x: 4 (x_hi: 2, x_lo: 2; x = x_hi * 2 + x_lo), y: 4, z: 8, core: 2. Of those that a mesh axis runs over, the one named last changes fastest.
Arguments:
- tokens: bfloat16 [131072, 2048], P(('replica', 'fsdp')), may hold values from -30 to 30
- cotangent: bfloat16 [131072, 512], P(('replica', 'fsdp')), may hold values from -6 to 6
- step_count: int32 [1], replicated, may hold values from 1 to 8
- master: float32 [64, 512, 2048], P('replica', 'fsdp'), may hold values from -16 to 16
- first_moment_adamw: float32 [64, 512, 2048], P('replica', 'fsdp'), may hold values from -6 to 6
- moment_second: float32 [64, 512, 2048], P('replica', 'fsdp'), may hold values from 0.05 to 5
- anchor: float32 [512, 2048], P('fsdp', 'replica'), may hold values from -6 to 6
- outer_moment: float32 [512, 2048], P('fsdp', 'replica'), may hold values from -3 to 3
- pending: float32 [512, 2048], P('fsdp', 'replica'), may hold values from -3 to 3
Outputs:
- key_out: bfloat16 [131072, 512], P(('replica', 'fsdp'))
- input_grad: bfloat16 [131072, 2048], P(('replica', 'fsdp'))
- params: float32 [64, 512, 2048], P('replica', 'fsdp')
- moment_first_new: float32 [64, 512, 2048], P('replica', 'fsdp')
- moment_second_new: float32 [64, 512, 2048], P('replica', 'fsdp')
- anchor_new: float32 [512, 2048], P('fsdp', 'replica')
- outer_moment_new: float32 [512, 2048], P('fsdp', 'replica')
- pending_new: float32 [512, 2048], P('fsdp', 'replica')
All inputs are finite; a program needn't handle non-finite values.
Results may differ from a plain program's by a relative error of at most 0.0058.
Values may be sent and summed in bfloat16 or wider, within the bound.
A program may use at most 64 MiB of HBM per device.

v0:
```python
import math

import jax
import jax.numpy as jnp
from jax import lax
from jax.sharding import PartitionSpec as P

HEAD_DIM = 64


ROPE_BASE = 500000.0
EPS_NORM = 1e-05
BETA_ONE = 0.9
BETA_TWO = 0.95
EPS_ADAM = 1e-08
LEARN_RATE = 0.1
WEIGHT_DECAY = 0.1
OUTER_RATE = 0.7
OUTER_MOMENTUM = 0.9
MIX_LOCAL = 0.5


def rope_tables(positions, col_count, head_size):
    column = jnp.arange(col_count) % head_size % (head_size // 2)
    exponent = 2.0 * column.astype(jnp.float32) / head_size
    inverse_freq = jnp.exp(-exponent * math.log(ROPE_BASE))
    angles = positions[:, None] * inverse_freq[None, :]
    return (jnp.cos(angles), jnp.sin(angles))


def rotate_half(values, head_size):
    row_count, col_count = values.shape
    halves = values.reshape(row_count, col_count // head_size, 2, head_size // 2)
    turned = jnp.concatenate([-halves[:, :, 1:2], halves[:, :, 0:1]], axis=2)
    return turned.reshape(row_count, col_count)


def norm_forward(tokens):
    floats = tokens.astype(jnp.float32)
    inverse = lax.rsqrt(jnp.mean(floats * floats, axis=-1, keepdims=True) + EPS_NORM)
    return (floats, inverse)


def norm_backward(floats, inverse, hidden_grad):
    inner_sum = jnp.mean(hidden_grad * floats, axis=-1, keepdims=True)
    return (inverse * hidden_grad - floats * inverse**3 * inner_sum).astype(jnp.bfloat16)


def adam_update(weights, gradient, moment_one, moment_two, bias_one, bias_two):
    moment_one_new = BETA_ONE * moment_one + (1.0 - BETA_ONE) * gradient
    moment_two_new = BETA_TWO * moment_two + (1.0 - BETA_TWO) * gradient * gradient
    update = moment_one_new / bias_one / (jnp.sqrt(moment_two_new / bias_two) + EPS_ADAM)
    return (
        weights - LEARN_RATE * (update + WEIGHT_DECAY * weights),
        moment_one_new,
        moment_two_new,
    )


def outer_merge(anchor, outer_moment, pending):
    outer_moment_new = OUTER_MOMENTUM * outer_moment + pending
    anchor_new = anchor - OUTER_RATE * (pending + OUTER_MOMENTUM * outer_moment_new)
    return (anchor_new, outer_moment_new)


def on_device(
    tokens,
    cotangent,
    step_count,
    master,
    first_moment_adamw,
    moment_second,
    anchor,
    outer_moment,
    pending,
):
    row_count = tokens.shape[0]
    key_width = cotangent.shape[1]
    scale_factor = 1.0 / math.sqrt(tokens.shape[1])
    positions = jnp.arange(row_count).astype(jnp.float32)
    cosine, sine_table = rope_tables(positions, key_width, HEAD_DIM)
    floats, inverse = norm_forward(tokens)
    normalized_input = (floats * inverse).astype(jnp.bfloat16)
    weights_local = master[0]
    weights_half = weights_local.astype(jnp.bfloat16)
    cot_float = cotangent.astype(jnp.float32)
    key_gradient = (
        (cot_float * cosine - rotate_half(cot_float * sine_table, HEAD_DIM)) * scale_factor
    ).astype(jnp.bfloat16)
    contract_rows = (((1,), (1,)), ((), ()))
    weights_full = lax.all_gather(weights_half, "fsdp", axis=0, tiled=True)
    projected = lax.dot_general(
        normalized_input, weights_full, contract_rows, preferred_element_type=jnp.float32
    )
    hidden_grad = jnp.dot(key_gradient, weights_full, preferred_element_type=jnp.float32)
    projected = projected * scale_factor
    key_out = (projected * cosine + rotate_half(projected, HEAD_DIM) * sine_table).astype(
        jnp.bfloat16
    )
    input_grad = norm_backward(floats, inverse, hidden_grad)
    gradient = lax.psum_scatter(
        lax.dot_general(
            key_gradient,
            normalized_input,
            (((0,), (0,)), ((), ())),
            preferred_element_type=jnp.float32,
        ).astype(jnp.bfloat16),
        "fsdp",
        scatter_dimension=0,
        tiled=True,
    ).astype(jnp.float32)
    steps_float = step_count[0].astype(jnp.float32)
    bias_one = 1.0 - jnp.power(jnp.float32(BETA_ONE), steps_float)
    bias_two = 1.0 - jnp.power(jnp.float32(BETA_TWO), steps_float)
    inner, moment_one_new, moment_two_new = adam_update(
        weights_local, gradient, first_moment_adamw[0], moment_second[0], bias_one, bias_two
    )
    merged, moment_next = outer_merge(anchor, outer_moment, pending)
    merged_full = lax.all_gather(merged, "replica", axis=1, tiled=True)
    replica_count = lax.axis_size("replica")
    summed_inner = lax.psum_scatter(inner, "replica", scatter_dimension=1, tiled=True)
    pending_new = anchor - summed_inner / replica_count
    params = MIX_LOCAL * inner + (1.0 - MIX_LOCAL) * merged_full
    return (
        key_out,
        input_grad,
        params[None],
        moment_one_new[None],
        moment_two_new[None],
        merged,
        moment_next,
        pending_new,
    )


def solution(mesh):
    in_specs = (
        P(("replica", "fsdp"), None),
        P(("replica", "fsdp"), None),
        P(),
        P("replica", "fsdp", None),
        P("replica", "fsdp", None),
        P("replica", "fsdp", None),
        P("fsdp", "replica"),
        P("fsdp", "replica"),
        P("fsdp", "replica"),
    )
    out_specs = (
        P(("replica", "fsdp"), None),
        P(("replica", "fsdp"), None),
        P("replica", "fsdp", None),
        P("replica", "fsdp", None),
        P("replica", "fsdp", None),
        P("fsdp", "replica"),
        P("fsdp", "replica"),
        P("fsdp", "replica"),
    )
    return jax.shard_map(
        on_device, mesh=mesh, in_specs=in_specs, out_specs=out_specs, check_vma=False
    )
```

profile of v0, /device:TPU:4, one launch (start us, length us, event | category | flops | bytes accessed | tf_op | source)
XLA Modules:
  0.0 714.1 jit_solution(13545953133598692457)
XLA Ops:
  7.2 0.0 all-gather.3.cloned.1.call-start
  7.3 2.1 bitcast_convert_fusion
  9.4 0.0 all-gather.5.cloned.1.call-start
  9.5 0.6 multiply_subtract_fusion.1
  10.1 0.0 all-gather.5.cloned.1.call-update
  10.2 0.0 reduce-scatter.5.cloned.1.call-start
  10.2 0.2 copy.27
  10.5 3.5 fusion.8
  14.0 0.1 slice_negate_fusion
  14.1 0.1 pad_maximum_fusion.1
  14.2 4.0 fusion.15
  18.2 21.7 %all-gather.3.cloned.1.call-done = bf16[512,2048]{1,0:T(8,128)(2,1)} async-done(((bf16[128,2048]{1,0:T(8,128)(2,1)}), bf16[512,2048]{1,0:T(8,128)(2,1)}) %all-gather.3.cloned.1.call-update) | async-done | bytes 2097168 | tf_op jit(solution)/shard_map/all_gather | solution.py:91
  39.9 5.1 fusion.5
  45.0 2.7 convolution_convert_fusion
  47.7 0.0 reduce-scatter.5.cloned.1.call-update
  47.7 0.2 reduce-scatter.7.cloned.1.call-start
  48.7 292.1 %all-gather.5.cloned.1.call-done = f32[128,2048]{0,1:T(8,128)} async-done(((f32[128,32]{0,1:T(8,128)}), f32[128,2048]{0,1:T(8,128)}) %all-gather.5.cloned.1.call-update) | async-done | bytes 1048592 | tf_op jit(solution)/shard_map/all_gather | solution.py:119
  340.8 1.6 copy.28
  342.4 40.6 %reduce-scatter.5.cloned.1.call-done = bf16[128,2048]{1,0:T(8,128)(2,1)} async-done(((bf16[512,2048]{1,0:T(8,128)(2,1)}), bf16[128,2048]{1,0:T(8,128)(2,1)}) %reduce-scatter.5.cloned.1.call-update) | async-done | bytes 524304 | tf_op jit(solution)/shard_map/reduce_scatter | solution.py:101
  383.0 4.0 multiply_bitcast_fusion
  387.0 1.3 copy.32
  388.4 0.1 copy.29
  388.4 0.5 copy-done.2
  389.0 2.9 convolution_multiply_fusion
  391.9 0.1 slice_negate_fusion.1
  392.0 0.1 pad_maximum_fusion
  392.1 4.6 fusion.12
  396.8 1.0 copy.30
  397.8 4.3 fusion.4
  402.1 303.9 %reduce-scatter.7.cloned.1.call-done = f32[32,128]{1,0:T(8,128)} async-done(((f32[2048,128]{1,0:T(8,128)}), f32[32,128]{1,0:T(8,128)}) %reduce-scatter.7.cloned.1.call-update) | async-done | bytes 16400
  706.1 0.8 copy.33
  706.9 0.7 copy.31
  (22 shorter events, 0.1 us)
Async XLA Ops:
  7.2 2.3 copy-start.5
  7.2 2.3 copy-start.6
  7.2 2.3 copy-start.7
  7.2 3.0 copy-start.4
  7.2 32.7 %all-gather.3.cloned.1.call-start = ((), (), s32[]{:S(2)}) async-start(), calls=%async_computation.2 | async-start | bytes 2621440 | tf_op jit(solution)/shard_map/all_gather | solution.py:91
  9.4 331.4 %all-gather.5.cloned.1.call-start = ((), (), s32[]{:S(2)}) async-start(), calls=%async_computation.4 | async-start | bytes 1064960 | tf_op jit(solution)/shard_map/all_gather | solution.py:119
  10.2 372.9 %reduce-scatter.5.cloned.1.call-start = ((), (), s32[]{:S(2)}) async-start(), calls=%async_computation.3 | async-start | bytes 2621440 | tf_op jit(solution)/shard_map/reduce_scatter | solution.py:101
  14.1 25.8 %copy-start.1 = (bf16[512,2048]{1,0:T(8,128)(2,1)S(1)}, bf16[512,2048]{1,0:T(8,128)(2,1)}, u32[]{:S(2)}) copy-start(bf16[512,2048]{1,0:T(8,128)(2,1)} %param.9) | copy-start | bytes 6291460
  47.7 335.3 %copy-start = (f32[1,128,2048]{2,1,0:T(8,128)S(1)}, f32[1,128,2048]{2,1,0:T(8,128)}, u32[]{:S(2)}) copy-start(f32[1,128,2048]{2,1,0:T(8,128)} %param.12) | copy-start | bytes 3145732
  47.7 658.3 %reduce-scatter.7.cloned.1.call-start = ((), (), s32[]{:S(2)}) async-start(), calls=%async_computation.5 | async-start | bytes 1064960
  387.0 2.0 copy-start.2
  392.1 5.7 copy-start.3
Sparse Core Ops, SparseCore 0:
  10.4 29.4 all-gather.2
  42.3 298.5 all-gather.4
  344.2 38.7 reduce-scatter.4
  388.5 317.5 reduce-scatter.6
where the time goes:
time: 714 us
  waiting for transfers between devices  658 us (92%)
  other arithmetic  23.6 us (3%)
  between operations  14.7 us (2%)
  matrix products  10.7 us (1%)
    unnamed x5, waiting for transfers between devices  304 us
    all_gather x1, waiting for transfers between devices, on_device(): merged_full = lax.all_gather(merged, 'replica', axis=1, tiled=True)  292 us
    reduce_scatter x1, waiting for transfers between devices, on_device(): lax.psum_scatter(lax.dot_general(key_gradient, normalized_input, (((0,),...  40.6 us
    all_gather x1, waiting for transfers between devices, on_device(): weights_full = lax.all_gather(weights_half, 'fsdp', axis=0, tiled=True)  21.7 us
  transfers between devices with their start and end apart: 4, of which 4 were waited for; matrix products, arithmetic and copies ran while one was open for 4% of the time, Pallas kernels for 0%

commit v1 on v0

v1 whole, which is shorter than its diff:
```python
import math

import jax
import jax.numpy as jnp
import numpy as np
from jax import lax
from jax.experimental import pallas as pl
from jax.experimental.pallas import tpu as pltpu
from jax.sharding import PartitionSpec as P

MESH = pl.DeviceIdType.MESH
F32 = jnp.float32
BF16 = jnp.bfloat16

HEAD_DIM = 64
ROPE_BASE = 500000.0
EPS_NORM = 1e-05
BETA_ONE = 0.9
BETA_TWO = 0.95
EPS_ADAM = 1e-08
LEARN_RATE = 0.1
WEIGHT_DECAY = 0.1
OUTER_RATE = 0.7
OUTER_MOMENTUM = 0.9

TOK = 512
WIDTH = 2048
KEYS = 512
ROWS = 128
NZ, NY = 8, 4
CW = WIDTH // NZ
FEAT = 32
EARLY = 4
LAG = 3


def rope_tables():
    lane = np.arange(128)
    exponent = 2.0 * (lane % HEAD_DIM % (HEAD_DIM // 2)) / HEAD_DIM
    angles = np.arange(TOK)[:, None] * np.exp(-exponent * math.log(ROPE_BASE))[None, :]
    sign = np.where(lane % HEAD_DIM < HEAD_DIM // 2, -1.0, 1.0)[None, :]
    scale = 1.0 / math.sqrt(WIDTH)
    return (
        (np.cos(angles) * scale).astype(np.float32),
        (np.sin(angles) * sign * scale).astype(np.float32),
    )


def swap_halves(values):
    lane = lax.broadcasted_iota(jnp.int32, values.shape, 1)
    first = lax.rem(lane, HEAD_DIM) < HEAD_DIM // 2
    return jnp.where(first, pltpu.roll(values, 96, 1), pltpu.roll(values, 32, 1))


def step_kernel(
    stp, tok_h, cot_h, mas_h, m1_h, m2_h, anc_h, om_h, pen_h, cos_h, sin_h,
    tk, cs, sn, iv, pj, hd, acc, pv, m1n, m2n, smo,
    ct, ms, m1, m2, sm, nm, kg, kgt, wf, gb, rs, xs, xr, ib, rb, qs, qr, mt,
    ld,
    wss, wsr, wxs, wxr, wfs, wfr,
    gss, gsr, gxs, gxr, rzs, rzr, qss, qsr,
    a1, a2s, a2r, a3s, a3r,
):
    r = lax.axis_index("replica")
    f = lax.axis_index("fsdp")
    z = lax.div(r, 8)
    y = lax.rem(lax.div(r, 2), 4)
    xl = lax.rem(r, 2)
    core = lax.rem(f, 2)
    f_sib = f + 1 - 2 * core
    f_cross = lax.rem(f + 2, 4)
    f_diag = lax.rem(f_sib + 2, 4)
    sibling = (r, f_sib)
    cross = (r, f_cross)

    def at(zz, yy, xx):
        return ((zz * NY + yy) * 2 + xx, f)

    def z_peer(d):
        return lax.rem(z + d, NZ)

    def y_peer(d):
        return lax.rem(y + d, NY)

    def yx_peer(d):
        return y_peer(lax.div(d, 2)), lax.rem(xl + lax.rem(d, 2), 2)

    def chunk(i):
        half = lax.div(i + 1, 2)
        return lax.rem(z + 4 + (1 - 2 * lax.rem(i, 2)) * half, NZ)

    def rcopy(src, dst, send, recv, device):
        return pltpu.make_async_remote_copy(
            src_ref=src, dst_ref=dst, send_sem=send, recv_sem=recv,
            device_id=device, device_id_type=MESH,
        )

    def rank_rows(rank):
        return pl.ds(pl.multiple_of(rank * ROWS, ROWS), ROWS)

    def cols(c):
        return pl.ds(pl.multiple_of(c * CW, CW), CW)

    def w_sib(c, rank):
        block = wf.at[c, rank_rows(rank)]
        return rcopy(block, block, wss.at[c], wsr.at[c], sibling)

    def w_cross(c, rank):
        block = wf.at[c, rank_rows(rank)]
        return rcopy(block, block, wxs.at[c], wxr.at[c], cross)

    def w_fwd(c, rank):
        block = wf.at[c, rank_rows(rank)]
        return rcopy(block, block, wfs.at[c], wfr.at[c], sibling)

    def g_sib(c):
        return rcopy(
            gb.at[c, pl.ds(2 * ROWS, 2 * ROWS)], rs.at[c], gss.at[c], gsr.at[c], sibling
        )

    def g_cross(c):
        return rcopy(xs.at[c], xr.at[c], gxs.at[c], gxr.at[c], cross)

    def sum_z(c, slot):
        return rcopy(ib.at[c], rb.at[slot], rzs.at[c], rzr.at[slot], at(c, y, xl))

    def sum_yx(yy, xx, slot):
        part = yy * 2 + xx
        return rcopy(
            qs.at[pl.ds(pl.multiple_of(part * FEAT, FEAT), FEAT)], qr.at[slot],
            qss.at[part], qsr.at[slot], at(z, yy, xx),
        )

    def m_x(slot):
        block = mt.at[y, z, pl.ds(pl.multiple_of(slot * FEAT, FEAT), FEAT)]
        return rcopy(block, block, a1.at[0], a1.at[1], at(z, y, 1 - xl))

    def m_z(zz, slot):
        block = mt.at[y, slot]
        return rcopy(block, block, a2s.at[zz], a2r.at[slot], at(zz, y, xl))

    def m_y(yy, slot):
        block = mt.at[slot]
        return rcopy(block, block, a3s.at[yy], a3r.at[slot], at(z, yy, xl))

    loads = [
        pltpu.make_async_copy(mas_h, ms, ld.at[0]),
        pltpu.make_async_copy(anc_h, sm.at[0], ld.at[1]),
        pltpu.make_async_copy(om_h, sm.at[1], ld.at[2]),
        pltpu.make_async_copy(pen_h, sm.at[2], ld.at[3]),
        pltpu.make_async_copy(tok_h, tk, ld.at[4]),
        pltpu.make_async_copy(cot_h, ct, ld.at[5]),
        pltpu.make_async_copy(cos_h, cs, ld.at[6]),
        pltpu.make_async_copy(sin_h, sn, ld.at[7]),
        pltpu.make_async_copy(m1_h, m1, ld.at[8]),
        pltpu.make_async_copy(m2_h, m2, ld.at[9]),
    ]
    for load in loads:
        load.start()

    barrier = pltpu.get_barrier_semaphore()
    greeted = [sibling, cross, at(z, y, 1 - xl)]
    greeted += [at(z_peer(d), y, xl) for d in range(1, NZ)]
    greeted += [at(z, y_peer(d), xl) for d in range(1, NY)]
    greeted += [at(z, y_peer(d), 1 - xl) for d in range(1, NY)]
    for device in greeted:
        pl.semaphore_signal(barrier, inc=1, device_id=device, device_id_type=MESH)

    loads[0].wait()
    for c in range(NZ):
        wf[c, rank_rows(f), :] = ms[:, c * CW:(c + 1) * CW].astype(BF16)

    pl.semaphore_wait(barrier, len(greeted))

    for c in range(EARLY):
        w_cross(c, f).start()
    for c in range(NZ):
        w_sib(c, f).start()

    for k in (1, 2, 3):
        loads[k].wait()
    outer_new = OUTER_MOMENTUM * sm[1] + sm[2]
    anchor_new = sm[0] - OUTER_RATE * (sm[2] + OUTER_MOMENTUM * outer_new)
    smo[0] = anchor_new
    smo[1] = outer_new
    mt[y, z, pl.ds(pl.multiple_of(xl * FEAT, FEAT), FEAT), :] = anchor_new.astype(BF16)
    m_x(xl).start()

    loads[4].wait()

    @pl.loop(0, TOK // 16, unroll=2)
    def _(i):
        rows = pl.ds(pl.multiple_of(i * 16, 16), 16)
        x = tk[rows, :].astype(F32)
        inverse = lax.rsqrt(jnp.sum(x * x, axis=-1, keepdims=True) * (1.0 / WIDTH) + EPS_NORM)
        iv[rows, :] = jnp.broadcast_to(inverse, (16, 128))
        scaled = (x * inverse).astype(BF16)
        for c in range(NZ):
            nm[c, rows, :] = scaled[:, c * CW:(c + 1) * CW]

    m_x(1 - xl).wait_recv()
    for d in range(1, NZ):
        m_z(z_peer(d), z).start()

    for k in (5, 6, 7):
        loads[k].wait()

    @pl.loop(0, TOK // 64)
    def _(i):
        rows = pl.ds(pl.multiple_of(i * 64, 64), 64)
        cosine, sine = cs[rows, :], sn[rows, :]
        for b in range(KEYS // 128):
            v = ct[rows, b * 128:(b + 1) * 128].astype(F32)
            kg[rows, b * 128:(b + 1) * 128] = (v * cosine - swap_halves(v) * sine).astype(BF16)

    for k, rank in enumerate((f, f_cross, f_sib, f_diag)):
        kgt[k * ROWS:(k + 1) * ROWS, :] = kg[:, rank_rows(rank)].astype(F32).T.astype(BF16)

    @pl.loop(0, NZ + LAG)
    def _(i):
        @pl.when(i < NZ)
        def _():
            c = chunk(i)
            gb[c] = jnp.dot(kgt[...], nm[c], preferred_element_type=F32).astype(BF16)
            g_sib(c).start()

        @pl.when(i >= LAG)
        def _():
            c = chunk(i - LAG)
            g_sib(c).wait_recv()
            xs[c] = (
                gb[c, ROWS:2 * ROWS, :].astype(F32) + rs[c, ROWS:2 * ROWS, :].astype(F32)
            ).astype(BF16)
            g_cross(c).start()

        @pl.when(lax.rem(i, 3) == 1)
        def _():
            c = lax.div(i, 3)
            w_cross(c, f_cross).wait_recv()
            w_fwd(c, f_cross).start()

    for d in range(1, NZ):
        m_z(z, z_peer(d)).wait_recv()
    for d in range(1, NY):
        m_y(y_peer(d), y).start()

    pj[...] = jnp.zeros_like(pj)
    acc[...] = jnp.zeros_like(acc)

    def use_weights(c):
        w_sib(c, f_sib).wait_recv()
        w_fwd(c, f_diag).wait_recv()

        @pl.loop(0, 2)
        def _(i):
            rows = pl.ds(pl.multiple_of(i * 256, 256), 256)
            w = wf[c]
            pj[rows, :] += lax.dot_general(
                nm[c, rows, :], w, (((1,), (1,)), ((), ())), preferred_element_type=F32
            )
            hidden = jnp.dot(kg[rows, :], w, preferred_element_type=F32)
            hd[c, rows, :] = hidden
            product = hidden * tk[rows, cols(c)].astype(F32)
            acc[rows, :] += product[:, :128] + product[:, 128:]

    for k in (8, 9):
        loads[k].wait()
    steps = jnp.full((8, 128), stp[0], jnp.int32).astype(F32)
    inverse_one = (1.0 / (1.0 - jnp.exp(steps * math.log(BETA_ONE))))[0:1, 0:1]
    inverse_two = (1.0 / (1.0 - jnp.exp(steps * math.log(BETA_TWO))))[0:1, 0:1]

    @pl.loop(0, NZ)
    def _(i):
        c = chunk(i)
        g_cross(c).wait_recv()

        @pl.loop(0, ROWS // 32)
        def _(k):
            rows = pl.ds(pl.multiple_of(k * 32, 32), 32)
            g = (gb[c, rows, :].astype(F32) + rs[c, rows, :].astype(F32)) + xr[c, rows, :].astype(F32)
            one = BETA_ONE * m1[rows, cols(c)] + (1.0 - BETA_ONE) * g
            two = BETA_TWO * m2[rows, cols(c)] + (1.0 - BETA_TWO) * g * g
            m1n[rows, cols(c)] = one
            m2n[rows, cols(c)] = two
            update = (one * inverse_one) / (jnp.sqrt(two * inverse_two) + EPS_ADAM)
            master = ms[rows, cols(c)]
            inner = master - LEARN_RATE * (update + WEIGHT_DECAY * master)
            pv[rows, cols(c)] = inner
            ib[c, rows, :] = inner.astype(BF16)

        @pl.when(i < NZ - 1)
        def _():
            sum_z(c, z).start()

        @pl.when(i >= 5)
        def _():
            w_cross(i - 1, f).start()

        @pl.when(i == 7)
        def _():
            w_cross(7, f).start()

        @pl.when(i < EARLY)
        def _():
            use_weights(i)

    for d in range(1, NY):
        m_y(y, y_peer(d)).wait_recv()

    @pl.loop(0, NZ)
    def _(c):
        merged = mt[:, c].astype(F32).reshape(CW, ROWS).T
        pv[:, cols(c)] = 0.5 * pv[:, cols(c)] + 0.5 * merged

    def forward(c):
        w_cross(c, f_cross).wait_recv()
        w_fwd(c, f_cross).start()

    forward(4)

    total = ib[z].astype(F32)
    for d in range(1, NZ):
        sum_z(z, z_peer(d)).wait_recv()
        total = total + rb[z_peer(d)].astype(F32)
    total = total.T
    qs[...] = total.astype(BF16)
    for d in range(1, 8):
        yy, xx = yx_peer(d)
        sum_yx(yy, xx, y * 2 + xl).start()

    @pl.loop(5, NZ)
    def _(c):
        forward(c)
        use_weights(c - 1)

    own = y * 2 + xl
    total = qs[pl.ds(pl.multiple_of(own * FEAT, FEAT), FEAT), :].astype(F32)
    for d in range(1, 8):
        yy, xx = yx_peer(d)
        sum_yx(y, xl, yy * 2 + xx).wait_recv()
        total = total + qr[yy * 2 + xx].astype(F32)
    smo[2] = sm[0] - total * (1.0 / 64.0)

    use_weights(NZ - 1)

    @pl.loop(0, NZ)
    def _(c):
        w_sib(c, f).wait_send()
        w_cross(c, f).wait_send()
        w_fwd(c, f_cross).wait_send()
        g_sib(c).wait_send()
        g_cross(c).wait_send()

    for d in range(1, NZ):
        sum_z(z_peer(d), z).wait_send()
        m_z(z_peer(d), z).wait_send()
    for d in range(1, 8):
        yy, xx = yx_peer(d)
        sum_yx(yy, xx, y * 2 + xl).wait_send()
    for d in range(1, NY):
        m_y(y_peer(d), y).wait_send()
    m_x(xl).wait_send()

def finish_kernel(
    tk, cs, sn, iv, pj, hd, acc, pv, m1n, m2n, smo,
    key_h, ing_h, par_h, m1n_h, m2n_h, ancn_h, omn_h, penn_h,
    igv, kov, st,
):
    whole = [
        pltpu.make_async_copy(m1n, m1n_h, st.at[0]),
        pltpu.make_async_copy(m2n, m2n_h, st.at[1]),
        pltpu.make_async_copy(pv, par_h, st.at[2]),
        pltpu.make_async_copy(smo.at[0], ancn_h, st.at[3]),
        pltpu.make_async_copy(smo.at[1], omn_h, st.at[4]),
        pltpu.make_async_copy(smo.at[2], penn_h, st.at[5]),
    ]
    for copy in whole:
        copy.start()

    @pl.loop(0, TOK // 128)
    def _(j):
        @pl.loop(0, 4)
        def _(k):
            rows = pl.ds(pl.multiple_of(j * 128 + k * 32, 32), 32)
            inverse = iv[rows, :]
            mean = jnp.sum(acc[rows, :], axis=-1, keepdims=True) * (1.0 / WIDTH)
            coef = inverse * inverse * inverse * mean
            for c in range(NZ):
                for b in range(2):
                    left = c * CW + b * 128
                    igv[rows, left:left + 128] = (
                        inverse * hd[c, rows, b * 128:(b + 1) * 128]
                        - tk[rows, left:left + 128].astype(F32) * coef
                    ).astype(BF16)

        rows = pl.ds(pl.multiple_of(j * 128, 128), 128)
        pltpu.make_async_copy(igv.at[rows], ing_h.at[rows], st.at[6]).start()

    @pl.loop(0, TOK // 64)
    def _(i):
        rows = pl.ds(pl.multiple_of(i * 64, 64), 64)
        cosine, sine = cs[rows, :], sn[rows, :]
        for b in range(KEYS // 128):
            v = pj[rows, b * 128:(b + 1) * 128]
            kov[rows, b * 128:(b + 1) * 128] = (v * cosine + swap_halves(v) * sine).astype(BF16)

    keys_out = pltpu.make_async_copy(kov, key_h, st.at[7])
    keys_out.start()
    for copy in whole:
        copy.wait()
    pltpu.make_async_copy(igv, ing_h, st.at[6]).wait()
    keys_out.wait()


def on_device(
    tokens, cotangent, step_count, master, first_moment, moment_second,
    anchor, outer_moment, pending,
):
    cosine, sine = rope_tables()
    any_spec = pl.BlockSpec(memory_space=pl.ANY)
    vmem_spec = pl.BlockSpec(memory_space=pltpu.VMEM)
    vmem = pltpu.VMEM
    dma = pltpu.SemaphoreType.DMA
    shape = jax.ShapeDtypeStruct
    inputs = (
        tokens, cotangent, master[0], first_moment[0], moment_second[0],
        anchor.T, outer_moment.T, pending.T, jnp.asarray(cosine), jnp.asarray(sine),
    )
    inputs = [pltpu.with_memory_space_constraint(x, pltpu.HBM) for x in inputs]
    held = pl.pallas_call(
        step_kernel,
        out_shape=(
            shape((TOK, WIDTH), BF16),
            shape((TOK, 128), F32),
            shape((TOK, 128), F32),
            shape((TOK, 128), F32),
            shape((TOK, KEYS), F32),
            shape((NZ, TOK, CW), F32),
            shape((TOK, 128), F32),
            shape((ROWS, WIDTH), F32),
            shape((ROWS, WIDTH), F32),
            shape((ROWS, WIDTH), F32),
            shape((3, FEAT, ROWS), F32),
        ),
        in_specs=[pl.BlockSpec(memory_space=pltpu.SMEM)] + [any_spec] * 10,
        out_specs=(vmem_spec,) * 11,
        scratch_shapes=[
            vmem((TOK, KEYS), BF16),
            vmem((ROWS, WIDTH), F32),
            vmem((ROWS, WIDTH), F32),
            vmem((ROWS, WIDTH), F32),
            vmem((3, FEAT, ROWS), F32),
            vmem((NZ, TOK, CW), BF16),
            vmem((TOK, KEYS), BF16),
            vmem((KEYS, TOK), BF16),
            vmem((NZ, KEYS, CW), BF16),
            vmem((NZ, KEYS, CW), BF16),
            vmem((NZ, 2 * ROWS, CW), BF16),
            vmem((NZ, ROWS, CW), BF16),
            vmem((NZ, ROWS, CW), BF16),
            vmem((NZ, ROWS, CW), BF16),
            vmem((NZ, ROWS, CW), BF16),
            vmem((CW, ROWS), BF16),
            vmem((8, FEAT, ROWS), BF16),
            vmem((NY, NZ, 2 * FEAT, ROWS), BF16),
            dma((10,)),
            dma((NZ,)), dma((NZ,)), dma((NZ,)), dma((NZ,)), dma((NZ,)), dma((NZ,)),
            dma((NZ,)), dma((NZ,)), dma((NZ,)), dma((NZ,)),
            dma((NZ,)), dma((NZ,)), dma((8,)), dma((8,)),
            dma((2,)), dma((NZ,)), dma((NZ,)), dma((NY,)), dma((NY,)),
        ],
        compiler_params=pltpu.CompilerParams(
            collective_id=0, has_side_effects=True, vmem_limit_bytes=36 * 2**20
        ),
        name="step",
    )(step_count, *inputs)
    small = shape((FEAT, ROWS), F32)
    state = shape((ROWS, WIDTH), F32)
    outs = pl.pallas_call(
        finish_kernel,
        out_shape=(
            shape((TOK, KEYS), BF16), shape((TOK, WIDTH), BF16),
            state, state, state, small, small, small,
        ),
        in_specs=[vmem_spec] * 11,
        out_specs=(any_spec,) * 8,
        scratch_shapes=[vmem((TOK, WIDTH), BF16), vmem((TOK, KEYS), BF16), dma((8,))],
        compiler_params=pltpu.CompilerParams(vmem_limit_bytes=24 * 2**20),
        name="finish",
    )(*held)
    key_out, input_grad, params, one, two, anchor_new, outer_new, pending_new = outs
    return (
        key_out, input_grad, params[None], one[None], two[None],
        anchor_new.T, outer_new.T, pending_new.T,
    )


def solution(mesh):
    in_specs = (
        P(("replica", "fsdp"), None),
        P(("replica", "fsdp"), None),
        P(),
        P("replica", "fsdp", None),
        P("replica", "fsdp", None),
        P("replica", "fsdp", None),
        P("fsdp", "replica"),
        P("fsdp", "replica"),
        P("fsdp", "replica"),
    )
    out_specs = (
        P(("replica", "fsdp"), None),
        P(("replica", "fsdp"), None),
        P("replica", "fsdp", None),
        P("replica", "fsdp", None),
        P("replica", "fsdp", None),
        P("fsdp", "replica"),
        P("fsdp", "replica"),
        P("fsdp", "replica"),
    )
    return jax.shard_map(
        on_device, mesh=mesh, in_specs=in_specs, out_specs=out_specs, check_vma=False
    )
```

time: 714 us -> 48.9 us (0.07)
  the two profiles are of different devices: /device:TPU:4 before, /device:TPU:1 now
where the time goes in v1:
time: 48.9 us; the launch traced here: 48.8 us
  Pallas kernels  47.5 us (97%)
  between operations  1.29 us (3%)
    pallas_call x1, Pallas kernels, on_device(): pl.pallas_call(step_kernel, out_shape=(shape((TOK, WIDTH), BF16), shape((...  43.7 us
    pallas_call x1, Pallas kernels, on_device(): pl.pallas_call(finish_kernel, out_shape=(shape((TOK, KEYS), BF16), shape(...  3.82 us

profile of v1, /device:TPU:1, one launch (start us, length us, event | category | flops | bytes accessed | tf_op | source)
XLA Modules:
  0.0 48.8 jit_solution(8367443263516524105)
XLA Ops:
  1.3 43.7 %step.1 = (bf16[512,2048]{1,0:T(8,128)(2,1)S(1)}, f32[512,128]{1,0:T(8,128)S(1)}, f32[512,128]{1,0:T(8,128)S(1)}, f32[512,128]{1,0:T(8,128)S(1)}, f32[512,512]{1...) custom-call(s32[1]{0:T(128)S(6)} %copy.19.stp, ...), custom_call_target="tpu_custom_call" | custom-call | tf_op jit(solution)/shard_map/step/pallas_call | solution.py:430
  44.9 3.8 %finish.1 = (bf16[512,512]{1,0:T(8,128)(2,1)}, bf16[512,2048]{1,0:T(8,128)(2,1)}, f32[128,2048]{1,0:T(8,128)}, f32[128,2048]{1,0:T(8,128)}, f32[128,2048]{1,0:T(...) custom-call(bf16[512,2048]{1,0:T(8,128)(2,1)S(1)} %get-tuple-element.27.tk, ...), custom_call_target="tpu_custom_call" | custom-call | tf_op jit(solution)/shard_map/finish/pallas_call | solution.py:479

commit v2 on v1

--- a/solution.py
+++ b/solution.py
@@ -32,6 +32,7 @@
 FEAT = 32
 EARLY = 4
 LAG = 3
+LAG_Y = 2
 
 
 def rope_tables():
@@ -55,11 +56,11 @@
 def step_kernel(
     stp, tok_h, cot_h, mas_h, m1_h, m2_h, anc_h, om_h, pen_h, cos_h, sin_h,
     tk, cs, sn, iv, pj, hd, acc, pv, m1n, m2n, smo,
-    ct, ms, m1, m2, sm, nm, kg, kgt, wf, gb, rs, xs, xr, ib, rb, qs, qr, mt,
+    ct, ms, m1, m2, sm, nm, kg, kgt, wf, gb, rs, xs, xr, ib, yb, zs, zd, zo, qs, qr, mt,
     ld,
     wss, wsr, wxs, wxr, wfs, wfr,
-    gss, gsr, gxs, gxr, rzs, rzr, qss, qsr,
-    a1, a2s, a2r, a3s, a3r,
+    gss, gsr, gxs, gxr, yss, ysr, zss, zdr, qsem,
+    a1, a2s, a2r, a3s, a3r, ready,
 ):
     r = lax.axis_index("replica")
     f = lax.axis_index("fsdp")
@@ -76,18 +77,8 @@
     def at(zz, yy, xx):
         return ((zz * NY + yy) * 2 + xx, f)
 
-    def z_peer(d):
-        return lax.rem(z + d, NZ)
-
     def y_peer(d):
         return lax.rem(y + d, NY)
-
-    def yx_peer(d):
-        return y_peer(lax.div(d, 2)), lax.rem(xl + lax.rem(d, 2), 2)
-
-    def chunk(i):
-        half = lax.div(i + 1, 2)
-        return lax.rem(z + 4 + (1 - 2 * lax.rem(i, 2)) * half, NZ)
 
     def rcopy(src, dst, send, recv, device):
         return pltpu.make_async_remote_copy(
@@ -121,18 +112,22 @@
     def g_cross(c):
         return rcopy(xs.at[c], xr.at[c], gxs.at[c], gxr.at[c], cross)
 
+    def sum_y(c, yy, slot):
+        return rcopy(
+            ib.at[c, yy], yb.at[c, slot], yss.at[c, yy], ysr.at[c, slot], at(z, yy, xl)
+        )
+
     def sum_z(c, slot):
-        return rcopy(ib.at[c], rb.at[slot], rzs.at[c], rzr.at[slot], at(c, y, xl))
-
-    def sum_yx(yy, xx, slot):
-        part = yy * 2 + xx
-        return rcopy(
-            qs.at[pl.ds(pl.multiple_of(part * FEAT, FEAT), FEAT)], qr.at[slot],
-            qss.at[part], qsr.at[slot], at(z, yy, xx),
-        )
+        return rcopy(zs.at[c], zd.at[slot], zss.at[c], zdr.at[slot], at(c, y, xl))
+
+    def half(part):
+        return pl.ds(pl.multiple_of(part * FEAT, FEAT), FEAT)
+
+    def sum_x():
+        return rcopy(qs.at[half(1 - xl)], qr, qsem.at[0], qsem.at[1], at(z, y, 1 - xl))
 
     def m_x(slot):
-        block = mt.at[y, z, pl.ds(pl.multiple_of(slot * FEAT, FEAT), FEAT)]
+        block = mt.at[y, z, half(slot)]
         return rcopy(block, block, a1.at[0], a1.at[1], at(z, y, 1 - xl))
 
     def m_z(zz, slot):
@@ -155,27 +150,27 @@
         pltpu.make_async_copy(m1_h, m1, ld.at[8]),
         pltpu.make_async_copy(m2_h, m2, ld.at[9]),
     ]
-    for load in loads:
+    for load in loads[:8]:
         load.start()
 
     barrier = pltpu.get_barrier_semaphore()
-    greeted = [sibling, cross, at(z, y, 1 - xl)]
-    greeted += [at(z_peer(d), y, xl) for d in range(1, NZ)]
-    greeted += [at(z, y_peer(d), xl) for d in range(1, NY)]
-    greeted += [at(z, y_peer(d), 1 - xl) for d in range(1, NY)]
-    for device in greeted:
+
+    def greet(device):
         pl.semaphore_signal(barrier, inc=1, device_id=device, device_id_type=MESH)
+
+    greet(sibling)
+    greet(cross)
+    greet(at(z, y, 1 - xl))
+    for d in range(1, NY):
+        greet(at(z, y_peer(d), xl))
+    for t in range(NZ):
+        @pl.when(t > z)
+        def _():
+            greet(at(t, y, xl))
 
     loads[0].wait()
     for c in range(NZ):
         wf[c, rank_rows(f), :] = ms[:, c * CW:(c + 1) * CW].astype(BF16)
-
-    pl.semaphore_wait(barrier, len(greeted))
-
-    for c in range(EARLY):
-        w_cross(c, f).start()
-    for c in range(NZ):
-        w_sib(c, f).start()
 
     for k in (1, 2, 3):
         loads[k].wait()
@@ -183,10 +178,23 @@
     anchor_new = sm[0] - OUTER_RATE * (sm[2] + OUTER_MOMENTUM * outer_new)
     smo[0] = anchor_new
     smo[1] = outer_new
-    mt[y, z, pl.ds(pl.multiple_of(xl * FEAT, FEAT), FEAT), :] = anchor_new.astype(BF16)
+    mt[y, z, half(xl), :] = anchor_new.astype(BF16)
+
+    pl.semaphore_wait(barrier, 6 + z)
+    for t in range(NZ):
+        @pl.when(t < z)
+        def _():
+            pl.semaphore_signal(ready, inc=1, device_id=at(t, y, xl), device_id_type=MESH)
+
     m_x(xl).start()
+    for c in range(EARLY):
+        w_cross(c, f).start()
+    for c in range(NZ):
+        w_sib(c, f).start()
 
     loads[4].wait()
+    for load in loads[8:]:
+        load.start()
 
     @pl.loop(0, TOK // 16, unroll=2)
     def _(i):
@@ -199,8 +207,10 @@
             nm[c, rows, :] = scaled[:, c * CW:(c + 1) * CW]
 
     m_x(1 - xl).wait_recv()
-    for d in range(1, NZ):
-        m_z(z_peer(d), z).start()
+    for t in range(NZ):
+        @pl.when(t < z)
+        def _():
+            m_z(t, z).start()
 
     for k in (5, 6, 7):
         loads[k].wait()
@@ -220,29 +230,33 @@
     def _(i):
         @pl.when(i < NZ)
         def _():
-            c = chunk(i)
+            c = i
             gb[c] = jnp.dot(kgt[...], nm[c], preferred_element_type=F32).astype(BF16)
             g_sib(c).start()
 
         @pl.when(i >= LAG)
         def _():
-            c = chunk(i - LAG)
+            c = i - LAG
             g_sib(c).wait_recv()
             xs[c] = (
                 gb[c, ROWS:2 * ROWS, :].astype(F32) + rs[c, ROWS:2 * ROWS, :].astype(F32)
             ).astype(BF16)
             g_cross(c).start()
 
-        @pl.when(lax.rem(i, 3) == 1)
+        @pl.when((lax.rem(i, 3) == 1) & (i < 3 * EARLY))
         def _():
             c = lax.div(i, 3)
             w_cross(c, f_cross).wait_recv()
             w_fwd(c, f_cross).start()
 
-    for d in range(1, NZ):
-        m_z(z, z_peer(d)).wait_recv()
-    for d in range(1, NY):
-        m_y(y_peer(d), y).start()
+    @pl.when(z < NZ - 1)
+    def _():
+        pl.semaphore_wait(ready, NZ - 1 - z)
+
+    for t in range(NZ):
+        @pl.when(t > z)
+        def _():
+            m_z(t, z).start()
 
     pj[...] = jnp.zeros_like(pj)
     acc[...] = jnp.zeros_like(acc)
@@ -269,9 +283,11 @@
     inverse_one = (1.0 / (1.0 - jnp.exp(steps * math.log(BETA_ONE))))[0:1, 0:1]
     inverse_two = (1.0 / (1.0 - jnp.exp(steps * math.log(BETA_TWO))))[0:1, 0:1]
 
-    @pl.loop(0, NZ)
-    def _(i):
-        c = chunk(i)
+    def forward(c):
+        w_cross(c, f_cross).wait_recv()
+        w_fwd(c, f_cross).start()
+
+    def adam(c):
         g_cross(c).wait_recv()
 
         @pl.loop(0, ROWS // 32)
@@ -286,23 +302,75 @@
             master = ms[rows, cols(c)]
             inner = master - LEARN_RATE * (update + WEIGHT_DECAY * master)
             pv[rows, cols(c)] = inner
-            ib[c, rows, :] = inner.astype(BF16)
-
-        @pl.when(i < NZ - 1)
+
+        turned = pv[:, cols(c)].T.astype(BF16)
+        for k in range(NY):
+            ib[c, k] = turned[k * 2 * FEAT:(k + 1) * 2 * FEAT]
+        for d in range(1, NY):
+            sum_y(c, y_peer(d), y).start()
+
+    def pass_on(c):
+        total = ib[c, y].astype(F32)
+        for d in range(1, NY):
+            sum_y(c, y, y_peer(d)).wait_recv()
+            total = total + yb[c, y_peer(d)].astype(F32)
+        zs[c] = total.astype(BF16)
+
+        @pl.when(c == z)
+        def _():
+            zo[...] = total
+
+        @pl.when(c != z)
         def _():
             sum_z(c, z).start()
 
-        @pl.when(i >= 5)
-        def _():
-            w_cross(i - 1, f).start()
-
-        @pl.when(i == 7)
-        def _():
-            w_cross(7, f).start()
+    def sum_last():
+        for t in range(NZ):
+            @pl.when(t != z)
+            def _():
+                sum_z(z, t).wait_recv()
+                zo[...] += zd[t].astype(F32)
+        qs[...] = zo[...]
+        sum_x().start()
+
+    @pl.loop(0, 2 * NZ - EARLY)
+    def _(i):
+        @pl.when(i < NZ)
+        def _():
+            adam(i)
+
+        for k in range(3):
+            @pl.when(i == NZ - 3 + k)
+            def _():
+                for c in range(EARLY + k, NZ, 3):
+                    w_cross(c, f).start()
+
+        @pl.when(i == NZ - 1)
+        def _():
+            for t in range(NZ):
+                @pl.when(t != z)
+                def _():
+                    m_z(z, t).wait_recv()
+            for d in range(1, NY):
+                m_y(y_peer(d), y).start()
+
+        @pl.when(i >= NZ)
+        def _():
+            forward(i - NZ + EARLY)
 
         @pl.when(i < EARLY)
         def _():
             use_weights(i)
+
+        @pl.when(i > NZ)
+        def _():
+            use_weights(i - NZ + EARLY - 1)
+
+        @pl.when((i >= LAG_Y) & (i < NZ + LAG_Y))
+        def _():
+            pass_on(i - LAG_Y)
+
+    sum_last()
 
     for d in range(1, NY):
         m_y(y, y_peer(d)).wait_recv()
@@ -312,36 +380,10 @@
         merged = mt[:, c].astype(F32).reshape(CW, ROWS).T
         pv[:, cols(c)] = 0.5 * pv[:, cols(c)] + 0.5 * merged
 
-    def forward(c):
-        w_cross(c, f_cross).wait_recv()
-        w_fwd(c, f_cross).start()
-
-    forward(4)
-
-    total = ib[z].astype(F32)
-    for d in range(1, NZ):
-        sum_z(z, z_peer(d)).wait_recv()
-        total = total + rb[z_peer(d)].astype(F32)
-    total = total.T
-    qs[...] = total.astype(BF16)
-    for d in range(1, 8):
-        yy, xx = yx_peer(d)
-        sum_yx(yy, xx, y * 2 + xl).start()
-
-    @pl.loop(5, NZ)
-    def _(c):
-        forward(c)
-        use_weights(c - 1)
-
-    own = y * 2 + xl
-    total = qs[pl.ds(pl.multiple_of(own * FEAT, FEAT), FEAT), :].astype(F32)
-    for d in range(1, 8):
-        yy, xx = yx_peer(d)
-        sum_yx(y, xl, yy * 2 + xx).wait_recv()
-        total = total + qr[yy * 2 + xx].astype(F32)
-    smo[2] = sm[0] - total * (1.0 / 64.0)
-
     use_weights(NZ - 1)
+
+    sum_x().wait_recv()
+    smo[2] = sm[0] - (qs[half(xl), :] + qr[...]) * (1.0 / 64.0)
 
     @pl.loop(0, NZ)
     def _(c):
@@ -351,12 +393,15 @@
         g_sib(c).wait_send()
         g_cross(c).wait_send()
 
-    for d in range(1, NZ):
-        sum_z(z_peer(d), z).wait_send()
-        m_z(z_peer(d), z).wait_send()
-    for d in range(1, 8):
-        yy, xx = yx_peer(d)
-        sum_yx(yy, xx, y * 2 + xl).wait_send()
+    for c in range(NZ):
+        for d in range(1, NY):
+            sum_y(c, y_peer(d), y).wait_send()
+
+        @pl.when(c != z)
+        def _():
+            sum_z(c, z).wait_send()
+            m_z(c, z).wait_send()
+    sum_x().wait_send()
     for d in range(1, NY):
         m_y(y_peer(d), y).wait_send()
     m_x(xl).wait_send()
@@ -364,7 +409,7 @@
 def finish_kernel(
     tk, cs, sn, iv, pj, hd, acc, pv, m1n, m2n, smo,
     key_h, ing_h, par_h, m1n_h, m2n_h, ancn_h, omn_h, penn_h,
-    igv, kov, st,
+    igv, kov, co, st,
 ):
     whole = [
         pltpu.make_async_copy(m1n, m1n_h, st.at[0]),
@@ -377,14 +422,16 @@
     for copy in whole:
         copy.start()
 
+    mean = jnp.sum(acc[...], axis=-1, keepdims=True) * (1.0 / WIDTH)
+    co[...] = iv[...] * iv[...] * iv[...] * mean
+
     @pl.loop(0, TOK // 128)
     def _(j):
         @pl.loop(0, 4)
         def _(k):
             rows = pl.ds(pl.multiple_of(j * 128 + k * 32, 32), 32)
             inverse = iv[rows, :]
-            mean = jnp.sum(acc[rows, :], axis=-1, keepdims=True) * (1.0 / WIDTH)
-            coef = inverse * inverse * inverse * mean
+            coef = co[rows, :]
             for c in range(NZ):
                 for b in range(2):
                     left = c * CW + b * 128
@@ -458,16 +505,20 @@
             vmem((NZ, 2 * ROWS, CW), BF16),
             vmem((NZ, ROWS, CW), BF16),
             vmem((NZ, ROWS, CW), BF16),
-            vmem((NZ, ROWS, CW), BF16),
-            vmem((NZ, ROWS, CW), BF16),
-            vmem((CW, ROWS), BF16),
-            vmem((8, FEAT, ROWS), BF16),
+            vmem((NZ, NY, 2 * FEAT, ROWS), BF16),
+            vmem((NZ, NY, 2 * FEAT, ROWS), BF16),
+            vmem((NZ, 2 * FEAT, ROWS), BF16),
+            vmem((NZ, 2 * FEAT, ROWS), BF16),
+            vmem((2 * FEAT, ROWS), F32),
+            vmem((2 * FEAT, ROWS), F32),
+            vmem((FEAT, ROWS), F32),
             vmem((NY, NZ, 2 * FEAT, ROWS), BF16),
             dma((10,)),
             dma((NZ,)), dma((NZ,)), dma((NZ,)), dma((NZ,)), dma((NZ,)), dma((NZ,)),
             dma((NZ,)), dma((NZ,)), dma((NZ,)), dma((NZ,)),
-            dma((NZ,)), dma((NZ,)), dma((8,)), dma((8,)),
+            dma((NZ, NY)), dma((NZ, NY)), dma((NZ,)), dma((NZ,)), dma((2,)),
             dma((2,)), dma((NZ,)), dma((NZ,)), dma((NY,)), dma((NY,)),
+            pltpu.SemaphoreType.REGULAR,
         ],
         compiler_params=pltpu.CompilerParams(
             collective_id=0, has_side_effects=True, vmem_limit_bytes=36 * 2**20
@@ -484,7 +535,9 @@
         ),
         in_specs=[vmem_spec] * 11,
         out_specs=(any_spec,) * 8,
-        scratch_shapes=[vmem((TOK, WIDTH), BF16), vmem((TOK, KEYS), BF16), dma((8,))],
+        scratch_shapes=[
+            vmem((TOK, WIDTH), BF16), vmem((TOK, KEYS), BF16), vmem((TOK, 128), F32), dma((8,)),
+        ],
         compiler_params=pltpu.CompilerParams(vmem_limit_bytes=24 * 2**20),
         name="finish",
     )(*held)

time: 48.9 us -> 42 us (0.86)
  the two profiles are of different devices: /device:TPU:1 before, /device:TPU:226 now
where the time goes in v2:
time: 42 us; the launch traced here: 41.9 us
  Pallas kernels  40.6 us (97%)
  between operations  1.29 us (3%)
    pallas_call x1, Pallas kernels, on_device(): pl.pallas_call(step_kernel, out_shape=(shape((TOK, WIDTH), BF16), shape((...  37.6 us
    pallas_call x1, Pallas kernels, on_device(): pl.pallas_call(finish_kernel, out_shape=(shape((TOK, KEYS), BF16), shape(...  2.95 us

profile of v2, /device:TPU:226, one launch (start us, length us, event | category | flops | bytes accessed | tf_op | source)
XLA Modules:
  0.0 41.9 jit_solution(9204964083507854110)
XLA Ops:
  1.3 37.6 %step.1 = (bf16[512,2048]{1,0:T(8,128)(2,1)S(1)}, f32[512,128]{1,0:T(8,128)S(1)}, f32[512,128]{1,0:T(8,128)S(1)}, f32[512,128]{1,0:T(8,128)S(1)}, f32[512,512]{1...) custom-call(s32[1]{0:T(128)S(6)} %copy.19.stp, ...), custom_call_target="tpu_custom_call" | custom-call | tf_op jit(solution)/shard_map/step/pallas_call | solution.py:477
  38.9 3.0 %finish.1 = (bf16[512,512]{1,0:T(8,128)(2,1)}, bf16[512,2048]{1,0:T(8,128)(2,1)}, f32[128,2048]{1,0:T(8,128)}, f32[128,2048]{1,0:T(8,128)}, f32[128,2048]{1,0:T(...) custom-call(bf16[512,2048]{1,0:T(8,128)(2,1)S(1)} %get-tuple-element.27.tk, ...), custom_call_target="tpu_custom_call" | custom-call | tf_op jit(solution)/shard_map/finish/pallas_call | solution.py:530

commit v3 on v2

--- a/solution.py
+++ b/solution.py
@@ -340,7 +340,7 @@
             adam(i)
 
         for k in range(3):
-            @pl.when(i == NZ - 3 + k)
+            @pl.when(i == NZ - 5 + k)
             def _():
                 for c in range(EARLY + k, NZ, 3):
                     w_cross(c, f).start()

time: 42 us -> 41.6 us (level)
  no operation moved by 1% of the time
where the time goes in v3:
time: 41.6 us; the launch traced here: 41.5 us
  Pallas kernels  40.2 us (97%)
  between operations  1.29 us (3%)
    pallas_call x1, Pallas kernels, on_device(): pl.pallas_call(step_kernel, out_shape=(shape((TOK, WIDTH), BF16), shape((...  37.2 us
    pallas_call x1, Pallas kernels, on_device(): pl.pallas_call(finish_kernel, out_shape=(shape((TOK, KEYS), BF16), shape(...  2.95 us

profile of v3, /device:TPU:226, one launch (start us, length us, event | category | flops | bytes accessed | tf_op | source)
XLA Modules:
  0.0 41.5 jit_solution(741228710956861036)
XLA Ops:
  1.3 37.2 %step.1 = (bf16[512,2048]{1,0:T(8,128)(2,1)S(1)}, f32[512,128]{1,0:T(8,128)S(1)}, f32[512,128]{1,0:T(8,128)S(1)}, f32[512,128]{1,0:T(8,128)S(1)}, f32[512,512]{1...) custom-call(s32[1]{0:T(128)S(6)} %copy.19.stp, ...), custom_call_target="tpu_custom_call" | custom-call | tf_op jit(solution)/shard_map/step/pallas_call | solution.py:477
  38.5 3.0 %finish.1 = (bf16[512,512]{1,0:T(8,128)(2,1)}, bf16[512,2048]{1,0:T(8,128)(2,1)}, f32[128,2048]{1,0:T(8,128)}, f32[128,2048]{1,0:T(8,128)}, f32[128,2048]{1,0:T(...) custom-call(bf16[512,2048]{1,0:T(8,128)(2,1)S(1)} %get-tuple-element.27.tk, ...), custom_call_target="tpu_custom_call" | custom-call | tf_op jit(solution)/shard_map/finish/pallas_call | solution.py:530
